TPU v7x, 256 devices: a whole 4x4x8 slice. The times are simulated.
256 devices in a mesh: rows: 8 (over x_lo, y), pairs: 32 (over z, x_hi, core).
Axes of the slice: x: 4 (x_hi: 2, x_lo: 2; x = x_hi * 2 + x_lo), y: 4, z: 8, core: 2. Of those that a mesh axis runs over, the one named last changes fastest.
Arguments:
- matrix: float32 [32768, 8192], P('rows', 'pairs'), may hold values from -6 to 6
- vectors: float32 [8192, 8192], P('rows', 'pairs'), may hold values from -6 to 6
Outputs:
- matrix_out: float32 [32768, 8192], P('rows', 'pairs')
- vectors_out: float32 [8192, 8192], P('rows', 'pairs')
All inputs are finite; a program needn't handle non-finite values.
Results may differ from a plain program's by a relative error of at most 0.0029.
Values sent between devices are 32-bit elements; how exact they have to be, the bound alone decides.
A program may use at most 64 MiB of HBM per device.

v0:
```python
import jax
import jax.numpy as jnp
import numpy as np
from jax import lax
from jax.sharding import PartitionSpec as P

STEPS = 16
ROUNDS = 2


def shifted(block, axis, distance):
    devices = range(lax.axis_size(axis))
    route = [(i - distance, i) for i in devices if i - distance in devices]
    return lax.ppermute(block, axis, route)


def rotate_cols(block, cosine, sine, half):
    left = block[:, :half]
    right = block[:, half:]
    return jnp.concatenate([left * cosine + right * sine, right * cosine - left * sine], axis=1)


def rotate_rows(block, cosine, sine, half):
    upper = block[:half, :]
    lower = block[half:, :]
    cos_col = cosine[:, None]
    sin_col = sine[:, None]
    return jnp.concatenate(
        [upper * cos_col + lower * sin_col, lower * cos_col - upper * sin_col], axis=0
    )


def source_table(width):
    half = width // 2
    source = np.zeros(width, dtype=np.int64)
    source[0] = 0
    source[1] = half
    source[2:half] = np.arange(1, half - 1)
    source[half : width - 1] = np.arange(half + 1, width)
    source[width - 1] = half - 1
    return source


def selector(picks):
    width = picks.shape[0]
    table = np.zeros((width, width), dtype=np.float32)
    table[picks, np.arange(width)] = 1.0
    return jnp.asarray(table)


def exact_dot(left, right):
    return jnp.dot(left, right, precision=lax.Precision.HIGHEST, preferred_element_type=jnp.float32)


def jacobi(gram, steps):
    width = gram.shape[0]
    half = width // 2
    source = source_table(width)
    order = np.arange(width)
    for turn in range(steps):
        order = order[source]
    inverse = np.argsort(order)
    step_sel = selector(source)
    step_sel_t = jnp.transpose(step_sel)
    final_sel = selector(inverse)
    final_sel_t = jnp.transpose(final_sel)
    basis = jnp.eye(width, dtype=gram.dtype)

    def one_step(index, state):
        current, accum = state
        diag = jnp.diagonal(current)
        cross = jnp.diagonal(current[:half, half:])
        angle = 0.5 * jnp.arctan2(2.0 * cross, diag[:half] - diag[half:])
        cosine = jnp.cos(angle)
        sine = jnp.sin(angle)
        current = rotate_cols(current, cosine, sine, half)
        current = rotate_rows(current, cosine, sine, half)
        accum = rotate_cols(accum, cosine, sine, half)
        current = exact_dot(step_sel_t, exact_dot(current, step_sel))
        accum = exact_dot(accum, step_sel)
        return (current, accum)

    current, accum = lax.fori_loop(0, steps, one_step, (gram, basis))
    current = exact_dot(final_sel_t, exact_dot(current, final_sel))
    accum = exact_dot(accum, final_sel)
    return (current, accum)


def inner_products(left, right):
    return lax.dot_general(
        left,
        right,
        (((0,), (0,)), ((), ())),
        precision=lax.Precision.HIGHEST,
        preferred_element_type=jnp.float32,
    )


def full_gram(matrix):
    return lax.psum(inner_products(matrix, matrix), "rows")


def plain_moves(going_right, going_left):
    from_left = shifted((going_right[0], going_right[1]), "pairs", 1)
    from_right = shifted((going_left[0], going_left[1]), "pairs", -1)
    return (from_left, from_right)


def per_device(matrix, vectors):
    half = matrix.shape[1] // 2
    place = lax.axis_index("pairs")
    count = lax.axis_size("pairs")
    first = place == 0
    last = place == count - 1
    for turn in range(ROUNDS):
        gram = full_gram(matrix)
        rotated, basis = jacobi(gram, STEPS)
        matrix = exact_dot(matrix, basis)
        vectors = exact_dot(vectors, basis)
        top_a = matrix[:, :half]
        bottom_a = matrix[:, half:]
        top_v = vectors[:, :half]
        bottom_v = vectors[:, half:]
        send_a = jnp.where(first, bottom_a, top_a)
        send_v = jnp.where(first, bottom_v, top_v)
        from_left, from_right = plain_moves((send_a, send_v), (bottom_a, bottom_v))
        matrix = jnp.concatenate(
            [jnp.where(first, top_a, from_left[0]), jnp.where(last, top_a, from_right[0])], axis=1
        )
        vectors = jnp.concatenate(
            [jnp.where(first, top_v, from_left[1]), jnp.where(last, top_v, from_right[1])], axis=1
        )
    return (matrix, vectors)


def solution(mesh):
    in_specs = (P("rows", "pairs"), P("rows", "pairs"))
    out_specs = (P("rows", "pairs"), P("rows", "pairs"))
    return jax.shard_map(
        per_device, mesh=mesh, in_specs=in_specs, out_specs=out_specs, check_vma=False
    )
```

profile of v0, /device:TPU:68, one launch (start us, length us, event | category | flops | bytes accessed | tf_op | source)
XLA Modules:
  0.0 595.5 jit_solution(13937604050450460778)
XLA Ops:
  7.3 11.0 %fusion.58 = f32[256,256]{0,1:T(8,128)} fusion(f32[4096,256]{1,0:T(8,128)} %param.10), kind=kOutput, calls=%fused_computation.102 | convolution fusion | flops 3221225472 | bytes 4456448 | tf_op jit(solution)/shard_map/dot_general | solution.py:90
  18.6 80.8 %all-reduce.3.cloned.1.call-done = f32[256,256]{0,1:T(8,128)} async-done(((f32[256,256]{0,1:T(8,128)}), f32[256,256]{0,1:T(8,128)}) %all-reduce.3.cloned.1.call-update) | async-done | bytes 262160 | tf_op jit(solution)/shard_map/psum | solution.py:100
  99.4 123.0 %while.28 = (s32[]{:T(128)}, f32[256,256]{0,1:T(8,128)}, f32[256,256]{1,0:T(8,128)S(1)}, s32[]{:T(128)}, f32[256,256]{1,0:T(8,128)S(1)}, /*index=5*/f32[256,256]...) while((s32[]{:T(128)}, f32[256,256]{0,1:T(8,128)}, ...), condition=%wide.region_2.3_spmd.clone.clone, body=%wide.region_1.2_spmd.sunk.clone.clone.sunk | while | flops 604800896 | bytes 6438001 | solution.py:83
  99.4 2.7 gather_fusion
  107.1 2.6 gather_fusion
  114.8 2.6 gather_fusion
  122.5 2.6 gather_fusion
  130.2 2.6 gather_fusion
  137.9 2.6 gather_fusion
  145.6 2.6 gather_fusion
  153.2 2.6 gather_fusion
  160.9 2.6 gather_fusion
  168.6 2.6 gather_fusion
  176.3 2.6 gather_fusion
  199.4 2.6 gather_fusion
  207.1 2.6 gather_fusion
  214.8 2.6 gather_fusion
  222.8 8.6 %convolution_bitcast_fusion.2 = f32[4096,256]{0,1:T(8,128)S(1)} fusion(f32[256,256]{1,0:T(8,128)S(1)} %fusion.59, f32[4096,256]{1,0:T(8,128)} %param.10), kind=kOutput, calls=%fused_computation.72 | convolution fusion | flops 3221225472 | bytes 8650752 | tf_op jit(solution)/shard_map/dot_general | solution.py:52
  236.6 5.4 collective-permute-start.1
  242.0 2.8 convolution_bitcast_fusion.3
  244.8 41.5 %collective-permute-done = f32[4096,128]{0,1:T(8,128)} collective-permute-done((f32[4096,128]{0,1:T(8,128)}, f32[4096,128]{0,1:T(8,128)}, u32[]{:S(2)}, u32[]{:S(2)}) %collective-permute-start) | collective-permute-done | bytes 2097184 | tf_op jit(solution)/shard_map/ppermute | solution.py:14
  286.3 3.4 collective-permute-done.1
  289.7 3.3 slice_select_fusion.4
  295.0 4.2 fusion.47
  303.5 5.6 collective-permute-start.5
  309.1 71.3 %all-reduce.5.cloned.1.call-done = f32[256,256]{0,1:T(8,128)} async-done(((f32[256,256]{0,1:T(8,128)}), f32[256,256]{0,1:T(8,128)}) %all-reduce.5.cloned.1.call-update) | async-done | bytes 262160 | tf_op jit(solution)/shard_map/psum | solution.py:100
  380.4 123.3 %while.29 = (s32[]{:T(128)}, f32[256,256]{0,1:T(8,128)}, f32[256,256]{1,0:T(8,128)S(1)}, s32[]{:T(128)}, f32[256,256]{1,0:T(8,128)S(1)}, /*index=5*/f32[256,256]...) while((s32[]{:T(128)}, f32[256,256]{0,1:T(8,128)}, ...), condition=%wide.region_5.6_spmd.clone.clone, body=%wide.region_4.5_spmd.sunk.clone.clone.sunk | while | flops 604800896 | bytes 6438001 | solution.py:83
  380.5 2.7 gather_fusion.2
  388.2 2.6 gather_fusion.2
  395.9 2.6 gather_fusion.2
  403.6 2.6 gather_fusion.2
  411.3 2.6 gather_fusion.2
  426.7 2.6 gather_fusion.2
  434.4 2.6 gather_fusion.2
  442.1 2.6 gather_fusion.2
  449.8 2.6 gather_fusion.2
  457.5 2.6 gather_fusion.2
  465.2 2.6 gather_fusion.2
  472.9 2.6 gather_fusion.2
  480.6 2.6 gather_fusion.2
  488.3 2.6 gather_fusion.2
  496.1 2.6 gather_fusion.2
  504.1 5.6 fusion.46
  514.9 5.1 collective-permute-start.3
  524.6 5.1 collective-permute-start.7
  529.7 46.1 %collective-permute-done.6 = f32[1024,128]{0,1:T(8,128)S(1)} collective-permute-done((f32[1024,128]{0,1:T(8,128)S(1)}, f32[1024,128]{0,1:T(8,128)S(1)}, u32[]{:S(2)}, u32[]{:S(2)}) %collective-permute-start.6) | collective-permute-done | bytes 524320 | tf_op jit(solution)/shard_map/ppermute | solution.py:14
  577.3 3.3 slice_select_fusion.1
  583.1 5.6 copy.18
  (564 shorter events, 192.4 us)
Async XLA Ops:
  7.2 234.8 %copy-start = (f32[1024,256]{1,0:T(8,128)S(1)}, f32[1024,256]{1,0:T(8,128)}, u32[]{:S(2)}) copy-start(f32[1024,256]{1,0:T(8,128)} %param.11) | copy-start | bytes 3145732
  7.2 92.2 %copy-start.3 = (f32[256,256]{1,0:T(8,128)S(1)}, f32[256,256]{1,0:T(8,128)}, u32[]{:S(2)}) copy-start(f32[256,256]{1,0:T(8,128)} %constant.44.clone..sunk.6) | copy-start | bytes 786436
  7.2 92.2 %copy-start.4 = (f32[256,256]{0,1:T(8,128)S(1)}, f32[256,256]{0,1:T(8,128)}, u32[]{:S(2)}) copy-start(f32[256,256]{0,1:T(8,128)} %constant.235) | copy-start | bytes 786436
  7.2 92.2 %copy-start.7 = (f32[128,256]{1,0:T(8,128)S(1)}, f32[128,256]{1,0:T(8,128)}, u32[]{:S(2)}) copy-start(f32[128,256]{1,0:T(8,128)} %constant.236) | copy-start | bytes 393220
  7.2 92.1 %copy-start.8 = (f32[128,256]{1,0:T(8,128)S(1)}, f32[128,256]{1,0:T(8,128)}, u32[]{:S(2)}) copy-start(f32[128,256]{1,0:T(8,128)} %constant.237) | copy-start | bytes 393220
  7.2 92.1 %all-reduce.3.cloned.1.call-start = ((), (), s32[]{:S(2)}) async-start(), calls=%async_computation | async-start | bytes 524288 | tf_op jit(solution)/shard_map/psum | solution.py:100
  18.3 362.2 %all-reduce.5.cloned.1.call-start = ((), (), s32[]{:S(2)}) async-start(), calls=%async_computation.1 | async-start | bytes 524288 | tf_op jit(solution)/shard_map/psum | solution.py:100
  99.4 123.0 %copy-start.12 = (f32[256,256]{1,0:T(8,128)S(1)}, f32[256,256]{1,0:T(8,128)}, u32[]{:S(2)}) copy-start(f32[256,256]{1,0:T(8,128)} %constant.45.clone) | copy-start | bytes 786436
  99.4 4.9 copy-start.1
  107.1 4.9 copy-start.1
  114.8 4.9 copy-start.1
  122.5 4.9 copy-start.1
  130.2 4.9 copy-start.1
  137.8 4.9 copy-start.1
  145.5 4.9 copy-start.1
  153.2 4.9 copy-start.1
  160.9 4.9 copy-start.1
  168.6 4.9 copy-start.1
  176.3 4.9 copy-start.1
  184.0 4.9 copy-start.1
  191.7 4.9 copy-start.1
  199.4 4.9 copy-start.1
  207.0 4.9 copy-start.1
  214.7 4.9 copy-start.1
  234.7 51.6 %collective-permute-start = (f32[4096,128]{0,1:T(8,128)}, f32[4096,128]{0,1:T(8,128)}, u32[]{:S(2)}, u32[]{:S(2)}) collective-permute-start(f32[4096,128]{0,1:T(8,128)} %get-tuple-element.138), channel_id=1, source_target_pairs={{0,1},{1,2},{2,3},{3,4},{4,5},{5,6},{6,7},{7,8},{8,9},{9,10},{10,1... | collective-permute-start | bytes 6291464 | tf_op jit(solution)/shard_map/ppermute | solution.py:14
  236.6 53.1 %collective-permute-start.1 = (f32[4096,128]{0,1:T(8,128)}, f32[4096,128]{0,1:T(8,128)}, u32[]{:S(2)}, u32[]{:S(2)}) collective-permute-start(f32[4096,128]{0,1:T(8,128)} %get-tuple-element.139), channel_id=1, source_target_pairs={{1,0},{2,1},{3,2},{4,3},{5,4},{6,5},{7,6},{8,7},{9,8},{10,9},{11,1... | collective-permute-start | bytes 6291464 | tf_op jit(solution)/shard_map/ppermute | solution.py:14
  301.6 218.5 %collective-permute-start.4 = (f32[1024,128]{0,1:T(8,128)}, f32[1024,128]{0,1:T(8,128)}, u32[]{:S(2)}, u32[]{:S(2)}) collective-permute-start(f32[1024,128]{0,1:T(8,128)} %get-tuple-element.146), channel_id=1, source_target_pairs={{0,1},{1,2},{2,3},{3,4},{4,5},{5,6},{6,7},{7,8},{8,9},{9,10},{10,1... | collective-permute-start | bytes 1572872 | tf_op jit(solution)/shard_map/ppermute | solution.py:14
  303.5 216.6 %collective-permute-start.5 = (f32[1024,128]{0,1:T(8,128)}, f32[1024,128]{0,1:T(8,128)}, u32[]{:S(2)}, u32[]{:S(2)}) collective-permute-start(f32[1024,128]{0,1:T(8,128)} %get-tuple-element.147), channel_id=1, source_target_pairs={{1,0},{2,1},{3,2},{4,3},{5,4},{6,5},{7,6},{8,7},{9,8},{10,9},{11,1... | collective-permute-start | bytes 1572872 | tf_op jit(solution)/shard_map/ppermute | solution.py:14
  388.2 4.9 copy-start.2
  395.9 4.9 copy-start.2
  403.6 4.9 copy-start.2
  411.3 4.9 copy-start.2
  419.0 4.9 copy-start.2
  426.7 4.9 copy-start.2
  434.4 4.9 copy-start.2
  442.1 4.9 copy-start.2
  449.8 4.9 copy-start.2
  457.5 4.9 copy-start.2
  465.2 4.9 copy-start.2
  472.9 4.9 copy-start.2
  480.6 4.9 copy-start.2
  488.3 4.9 copy-start.2
  496.0 4.9 copy-start.2
  509.8 10.4 %copy-start.11 = (f32[1024,256]{0,1:T(8,128)S(1)}, f32[1024,256]{0,1:T(8,128)}, u32[]{:S(2)}) copy-start(f32[1024,256]{0,1:T(8,128)} %convolution_bitcast_fusion.3) | copy-start | bytes 3145732
  513.0 64.3 %collective-permute-start.2 = (f32[4096,128]{0,1:T(8,128)}, f32[4096,128]{0,1:T(8,128)}, u32[]{:S(2)}, u32[]{:S(2)}) collective-permute-start(f32[4096,128]{0,1:T(8,128)} %get-tuple-element.134), channel_id=1, source_target_pairs={{0,1},{1,2},{2,3},{3,4},{4,5},{5,6},{6,7},{7,8},{8,9},{9,10},{10,1... | collective-permute-start | bytes 6291464 | tf_op jit(solution)/shard_map/ppermute | solution.py:14
  514.9 62.4 %collective-permute-start.3 = (f32[4096,128]{0,1:T(8,128)}, f32[4096,128]{0,1:T(8,128)}, u32[]{:S(2)}, u32[]{:S(2)}) collective-permute-start(f32[4096,128]{0,1:T(8,128)} %get-tuple-element.135), channel_id=1, source_target_pairs={{1,0},{2,1},{3,2},{4,3},{5,4},{6,5},{7,6},{8,7},{9,8},{10,9},{11,1... | collective-permute-start | bytes 6291464 | tf_op jit(solution)/shard_map/ppermute | solution.py:14
  522.6 53.1 %collective-permute-start.6 = (f32[1024,128]{0,1:T(8,128)S(1)}, f32[1024,128]{0,1:T(8,128)S(1)}, u32[]{:S(2)}, u32[]{:S(2)}) collective-permute-start(f32[1024,128]{0,1:T(8,128)S(1)} %get-tuple-element.142), channel_id=1, source_target_pairs={{0,1},{1,2},{2,3},{3,4},{4,5},{5,6},{6,7},{7,8},{8,9},{9,10},{10,1... | collective-permute-start | bytes 1572872 | tf_op jit(solution)/shard_map/ppermute | solution.py:14
  524.6 51.2 %collective-permute-start.7 = (f32[1024,128]{0,1:T(8,128)S(1)}, f32[1024,128]{0,1:T(8,128)S(1)}, u32[]{:S(2)}, u32[]{:S(2)}) collective-permute-start(f32[1024,128]{0,1:T(8,128)S(1)} %get-tuple-element.143), channel_id=1, source_target_pairs={{1,0},{2,1},{3,2},{4,3},{5,4},{6,5},{7,6},{8,7},{9,8},{10,9},{11,1... | collective-permute-start | bytes 1572872 | tf_op jit(solution)/shard_map/ppermute | solution.py:14
  (5 other events, 14.8 us)
Sparse Core Ops, SparseCore 0:
  18.4 80.8 all-reduce.2
  299.4 80.9 all-reduce.4
where the time goes:
time: 600 us; the launch traced here: 596 us
  waiting for transfers between devices  243 us (40%)
  local copies, waits for them, and re-layouts  170 us (28%)
  matrix products  111 us (18%)
  starting transfers between devices  29.2 us (5%)
  other arithmetic  25.1 us (4%)
  between operations  14.4 us (2%)
    psum x2, waiting for transfers between devices, full_gram(): return lax.psum(inner_products(matrix, matrix), 'rows')  152 us
    dot_general x134, matrix products, exact_dot(): jnp.dot(left, right, precision=lax.Precision.HIGHEST, preferred_element_t...  95.7 us
    ppermute x8, waiting for transfers between devices, shifted(): return lax.ppermute(block, axis, route)  90.9 us
    gather x32, local copies, waits for them, and re-layouts, one_step(): diag = jnp.diagonal(current)  84.6 us
    gather x32, local copies, waits for them, and re-layouts, one_step(): cross = jnp.diagonal(current[:half, half:])  41 us
    ppermute x8, starting transfers between devices, shifted(): return lax.ppermute(block, axis, route)  28.9 us
    slice x32, local copies, waits for them, and re-layouts, one_step(): cross = jnp.diagonal(current[:half, half:])  27.1 us
    dot_general x2, matrix products, inner_products(): lax.dot_general(left, right, (((0,), (0,)), ((), ())), precision=lax.Prec...  15.2 us
  transfers between devices with their start and end apart: 10, of which 5 were waited for; matrix products, arithmetic and copies ran while one was open for 23% of the time, Pallas kernels for 0%

commit v1 on v0

v1 whole, which is shorter than its diff:
```python
import functools

import jax
import jax.numpy as jnp
from jax import lax
from jax.experimental import pallas as pl
from jax.experimental.pallas import tpu as pltpu
from jax.sharding import PartitionSpec as P

STEPS = 16
H = 128
W = 2 * H
CHUNK = 512
MESH = pl.DeviceIdType.MESH
F32 = jnp.float32
BF16 = jnp.bfloat16


def iota(shape, axis):
    return lax.broadcasted_iota(jnp.int32, shape, axis)


def split(v):
    hi = v.astype(BF16)
    return hi, (v - hi.astype(F32)).astype(BF16)


def split3(v):
    hi = v.astype(BF16)
    rest = v - hi.astype(F32)
    mid = rest.astype(BF16)
    return hi, mid, (rest - mid.astype(F32)).astype(BF16)


def dot(a, b):
    return jnp.dot(a, b, preferred_element_type=F32)


def dot_t(a, b):
    return lax.dot_general(a, b, (((0,), (0,)), ((), ())), preferred_element_type=F32)


def diag_row(block):
    lane = iota((8, H), 1)
    sub = iota((8, H), 0)
    parts = []
    for g in range(4):
        acc = block[32 * g : 32 * g + 8]
        for i in range(4 * g + 1, 4 * g + 4):
            acc = jnp.where(lane // 8 == i, block[8 * i : 8 * i + 8], acc)
        parts.append(acc)
    low = jnp.where(lane < 32, parts[0], parts[1])
    high = jnp.where(lane < 96, parts[2], parts[3])
    both = jnp.where(lane < 64, low, high)
    return jnp.sum(jnp.where(lane % 8 == sub, both, 0.0), axis=0, keepdims=True)


def angles(x, y):
    m = jnp.maximum(jnp.abs(x), jnp.abs(y))
    g = pl.reciprocal(m, approx=True)
    xs = x * g
    ys = y * g
    s = xs * xs + ys * ys
    r = s * lax.rsqrt(s)
    h = r + jnp.abs(xs)
    w = lax.rsqrt(2.0 * r * h)
    big = h * w
    small = jnp.abs(ys) * w
    flat = x >= 0.0
    none = m == 0.0
    cs = jnp.where(none, 1.0, jnp.where(flat, big, small))
    sn = jnp.where(none, 0.0, jnp.where(flat, small, big))
    return cs, jnp.where(y < 0.0, -sn, sn)


def lane_move(left, right):
    lane0 = iota(left.shape, 1) == 0
    rolled = pltpu.roll(jnp.where(lane0, right, left), 1, 1)
    new_left = jnp.where(lane0, left, rolled)
    new_right = pltpu.roll(jnp.where(lane0, rolled, right), H - 1, 1)
    return new_left, new_right


def as_columns(cs, sn):
    t = jnp.transpose(jnp.where(iota((H, H), 0) < H // 2, cs, sn))
    o = pltpu.roll(t, H // 2, 1)
    near = iota((H, H), 1) < H // 2
    return jnp.where(near, t, o), jnp.where(near, o, t)


def store_rows(ref, up, lo):
    ref[H - 1 : W - 1, :] = lo
    ref[1:H, :] = up[0 : H - 1]
    ref[0:1, :] = up[0:1]
    ref[1:2, :] = lo[0:1]
    ref[W - 1 : W, :] = up[H - 1 : H]


def jacobi_start(state, a, c, c_t, b):
    gl, gr, ql, qr = state
    gl[0:H, :] = a
    gl[H:W, :] = c_t
    gr[0:H, :] = c
    gr[H:W, :] = b
    ql[...] = (iota((W, H), 0) == iota((W, H), 1)).astype(F32)
    qr[...] = (iota((W, H), 0) == iota((W, H), 1) + H).astype(F32)


def jacobi_step(state):
    gl, gr, ql, qr = state
    a, d, c, b = gl[0:H], gl[H:W], gr[0:H], gr[H:W]
    cs, sn = angles(diag_row(a) - diag_row(b), 2.0 * diag_row(c))
    cc, sc = as_columns(cs, sn)
    a, c = lane_move(a * cs + c * sn, c * cs - a * sn)
    d, b = lane_move(d * cs + b * sn, b * cs - d * sn)
    store_rows(gl, a * cc + d * sc, d * cc - a * sc)
    store_rows(gr, c * cc + b * sc, b * cc - c * sc)
    left, right = ql[...], qr[...]
    left, right = lane_move(left * cs + right * sn, right * cs - left * sn)
    ql[...] = left
    qr[...] = right


def home():
    j = iota((W, W), 1)
    at = jnp.where(j < H - STEPS, j + STEPS, 3 * H - STEPS - 1 - j)
    at = jnp.where(j >= H, H + STEPS - j, at)
    at = jnp.where(j >= H + STEPS, j - STEPS, at)
    at = jnp.where(j == 0, 0, at)
    return (iota((W, W), 0) == at).astype(F32).astype(BF16)


def basis_split(state, sel):
    ql, qr = state[2], state[3]
    lh, ll = split(ql[...])
    rh, rl = split(qr[...])
    high = dot(lh, sel[0:H]) + dot(rh, sel[H:W])
    low = dot(ll, sel[0:H]) + dot(rl, sel[H:W])
    return high.astype(BF16), low.astype(BF16)


def gram_blocks(state, sel):
    gl, gr = state[0], state[1]
    moved = sum(dot(l, sel[0:H]) + dot(r, sel[H:W]) for l, r in zip(split3(gl[...]), split3(gr[...])))
    parts = split3(moved)
    top = sum(dot_t(sel[:, 0:H], p[:, 0:H]) for p in parts)
    bottom = sum(dot_t(sel[:, H:W], p[:, H:W]) for p in parts)
    return top, bottom


def kernel(
    n_rows, n_pairs, m_rows, v_rows,
    matrix, vectors, matrix_out, vectors_out,
    panel, mine, inbox, acc, gs, rs1, ag1, diag, rs2src, rs2, ag2,
    a_gl, a_gr, a_ql, a_qr, b_gl, b_gr, b_ql, b_qr,
    load_sem, out_sem, send_sem, recv_sem, rs1_send, rs1_recv, ag1_send, ag1_recv,
    dg_send, dg_recv, rs2_send, rs2_recv, ag2_send, ag2_recv,
):
    me = lax.axis_index("rows")
    k = lax.axis_index("pairs")
    first, second = k == 0, k == 1
    last, before_last = k == n_pairs - 1, k == n_pairs - 2
    m_chunks, v_chunks = m_rows // CHUNK, v_rows // CHUNK
    chunks = m_chunks + v_chunks
    piece = H // n_rows
    mine_rows = pl.ds(pl.multiple_of(me * piece, piece), piece)

    u_to = jnp.where(last, k - 1, jnp.where(before_last, k + 1, k + 2))
    u_slot = jnp.where(k >= n_pairs - 2, 1, 0)
    v_to = jnp.where(first, 1, jnp.where(second, 0, k - 2))
    v_slot = jnp.where(k <= 1, 0, 1)
    l_from, r_from = v_to, u_to

    def load(c):
        rows = pl.ds(pl.multiple_of(c * CHUNK, CHUNK), CHUNK)
        return pltpu.make_async_copy(matrix.at[rows], panel.at[rows], load_sem.at[c])

    def load_v(c):
        rows = pl.ds(pl.multiple_of(c * CHUNK, CHUNK), CHUNK)
        at = pl.ds(pl.multiple_of(m_rows + c * CHUNK, CHUNK), CHUNK)
        return pltpu.make_async_copy(vectors.at[rows], panel.at[at], load_sem.at[m_chunks + c])

    def each(n, body):
        lax.fori_loop(0, n, lambda i, carry: (body(i), carry)[1], 0)

    each(m_chunks, lambda c: load(c).start())
    each(v_chunks, lambda c: load_v(c).start())

    barrier = pltpu.get_barrier_semaphore()
    for d in range(1, n_rows):
        pl.semaphore_signal(barrier, inc=1, device_id=(lax.rem(me + d, n_rows), k), device_id_type=MESH)
    pl.semaphore_signal(barrier, inc=1, device_id=(me, l_from), device_id_type=MESH)
    pl.semaphore_signal(barrier, inc=1, device_id=(me, r_from), device_id_type=MESH)

    acc[...] = jnp.zeros_like(acc)

    def gram_chunk(c):
        load(c).wait()
        hi, lo = split(panel[pl.ds(pl.multiple_of(c * CHUNK, CHUNK), CHUNK), :])
        acc[0] += dot_t(hi, hi)
        acc[1] += dot_t(hi, lo)

    each(m_chunks, gram_chunk)
    hl = acc[1]
    full = acc[0] + (hl + jnp.transpose(hl))
    gs[:, 0:H] = full[0:H, 0:H]
    gs[:, H:W] = full[0:H, H:W]
    gs[:, W:] = full[H:W, H:W]

    pl.semaphore_wait(barrier, n_rows + 1)

    def peer(d):
        return lax.rem(me + d, n_rows)

    def scatter(src, dst, send, recv):
        copies = []
        for d in range(1, n_rows):
            rows = pl.ds(pl.multiple_of(peer(d) * piece, piece), piece)
            copies.append(
                pltpu.make_async_remote_copy(
                    src_ref=src.at[rows], dst_ref=dst.at[d], send_sem=send.at[d], recv_sem=recv.at[d],
                    device_id=(peer(d), k), device_id_type=MESH,
                )
            )
        for copy in copies:
            copy.start()
        for copy in copies:
            copy.wait()
        total = src[mine_rows, :]
        for d in range(1, n_rows):
            total = total + dst[d]
        return total

    def gather(buf, send, recv):
        copies = []
        for d in range(1, n_rows):
            copies.append(
                pltpu.make_async_remote_copy(
                    src_ref=buf.at[mine_rows], dst_ref=buf.at[mine_rows], send_sem=send.at[d], recv_sem=recv.at[d],
                    device_id=(peer(d), k), device_id_type=MESH,
                )
            )
        for copy in copies:
            copy.start()
        for copy in copies:
            copy.wait()

    ag1[mine_rows, :] = scatter(gs, rs1, rs1_send, rs1_recv)
    gather(ag1, ag1_send, ag1_recv)

    state_a = (a_gl, a_gr, a_ql, a_qr)
    state_b = (b_gl, b_gr, b_ql, b_qr)
    c1 = ag1[:, H:W]
    jacobi_start(state_a, ag1[:, 0:H], c1, jnp.transpose(c1), ag1[:, W:])
    each(STEPS, lambda t: jacobi_step(state_a))
    sel = home()
    q_hi, q_lo = basis_split(state_a, sel)

    def swapped(q):
        q = q.astype(F32)
        left = jnp.where(first, q[:, H:W], q[:, 0:H])
        right = jnp.where(first, q[:, 0:H], q[:, H:W])
        return left.astype(BF16), right.astype(BF16)

    qu_hi, qv_hi = swapped(q_hi)
    qu_lo, qv_lo = swapped(q_lo)
    q_hi = jnp.concatenate([qu_hi, qv_hi], axis=1)
    q_lo = jnp.concatenate([qu_lo, qv_lo], axis=1)

    def rows_of(c):
        return pl.ds(pl.multiple_of(c * CHUNK, CHUNK), CHUNK)

    def send(side, c):
        to, slot = ((u_to, u_slot), (v_to, v_slot))[side]
        return pltpu.make_async_remote_copy(
            src_ref=mine.at[side, rows_of(c)], dst_ref=inbox.at[slot, rows_of(c)],
            send_sem=send_sem.at[side, c], recv_sem=recv_sem.at[slot, c],
            device_id=(me, to), device_id_type=MESH,
        )

    def receive(slot, c):
        return pltpu.make_async_remote_copy(
            src_ref=mine.at[slot, rows_of(c)], dst_ref=inbox.at[slot, rows_of(c)],
            send_sem=send_sem.at[slot, c], recv_sem=recv_sem.at[slot, c],
            device_id=(me, u_to), device_id_type=MESH,
        )

    each(v_chunks, lambda c: load_v(c).wait())

    def rotate_chunk(c):
        hi, lo = split(panel[rows_of(c), :])
        new = dot(hi, q_hi) + (dot(hi, q_lo) + dot(lo, q_hi))
        mine[0, rows_of(c), :] = new[:, 0:H]
        mine[1, rows_of(c), :] = new[:, H:W]
        send(0, c).start()
        send(1, c).start()

    each(m_chunks, rotate_chunk)

    top, bottom = gram_blocks(state_a, sel)
    diag[0] = jnp.where(first, bottom, top)
    diag[1] = jnp.where(first, top, bottom)

    def send_diag(side):
        to, slot = ((u_to, u_slot), (v_to, v_slot))[side]
        return pltpu.make_async_remote_copy(
            src_ref=diag.at[side, mine_rows], dst_ref=ag2.at[2 + slot, mine_rows],
            send_sem=dg_send.at[side], recv_sem=dg_recv.at[slot],
            device_id=(me, to), device_id_type=MESH,
        )

    def receive_diag(slot):
        return pltpu.make_async_remote_copy(
            src_ref=diag.at[slot, mine_rows], dst_ref=ag2.at[2 + slot, mine_rows],
            send_sem=dg_send.at[slot], recv_sem=dg_recv.at[slot],
            device_id=(me, u_to), device_id_type=MESH,
        )

    send_diag(0).start()
    send_diag(1).start()
    lax.fori_loop(m_chunks, chunks, lambda c, carry: (rotate_chunk(c), carry)[1], 0)

    acc[...] = jnp.zeros_like(acc)

    def cross_chunk(c):
        receive(0, c).wait_recv()
        receive(1, c).wait_recv()
        for i, (x, y) in enumerate(((inbox[0, rows_of(c), :], mine[1, rows_of(c), :]),
                                    (mine[0, rows_of(c), :], inbox[1, rows_of(c), :]))):
            x = jnp.concatenate(split(x), axis=1)
            y = jnp.concatenate(split(y), axis=1)
            acc[i] += dot_t(x, y)

    each(m_chunks, cross_chunk)
    for i in range(2):
        z = acc[i]
        rs2src[:, i * H : (i + 1) * H] = z[0:H, 0:H] + ((z[0:H, H:W] + z[H:W, 0:H]) + z[H:W, H:W])
    total = scatter(rs2src, rs2, rs2_send, rs2_recv)
    ag2[0, mine_rows, :] = total[:, 0:H]
    ag2[1, mine_rows, :] = total[:, H:W]
    for side in range(2):
        send_diag(side).wait_send()
        receive_diag(side).wait_recv()

    copies = []
    for d in range(1, n_rows):
        copies.append(
            pltpu.make_async_remote_copy(
                src_ref=ag2.at[:, mine_rows], dst_ref=ag2.at[:, mine_rows],
                send_sem=ag2_send.at[d], recv_sem=ag2_recv.at[d],
                device_id=(peer(d), k), device_id_type=MESH,
            )
        )
    for copy in copies:
        copy.start()
    for copy in copies:
        copy.wait()

    xl, xr, dl, dr = ag2[0], ag2[1], ag2[2], ag2[3]
    xl_t, xr_t = jnp.transpose(xl), jnp.transpose(xr)
    du, dv = diag[0], diag[1]
    jacobi_start(
        state_a, jnp.where(first, dv, dl), jnp.where(first, xl_t, xl), jnp.where(first, xl, xl_t),
        jnp.where(first, dl, dv),
    )
    jacobi_start(
        state_b, jnp.where(last, dr, du), jnp.where(last, xr_t, xr), jnp.where(last, xr, xr_t),
        jnp.where(last, du, dr),
    )

    def both(t):
        jacobi_step(state_a)
        jacobi_step(state_b)

    each(STEPS, both)

    def weights(state, take_right, flip):
        parts = []
        for q in basis_split(state, sel):
            q = q.astype(F32)
            q = jnp.where(take_right, q[:, H:W], q[:, 0:H])
            up = jnp.where(flip, q[H:W], q[0:H])
            down = jnp.where(flip, q[0:H], q[H:W])
            parts.append(jnp.concatenate([up, down], axis=0).astype(BF16))
        return parts

    wl_hi, wl_lo = weights(state_a, second, first)
    wr_hi, wr_lo = weights(state_b, jnp.logical_not(last), jnp.logical_not(last))

    def finish_chunk(c):
        for i, (w_hi, w_lo) in enumerate(((wl_hi, wl_lo), (wr_hi, wr_lo))):
            x = jnp.concatenate([inbox[i, rows_of(c), :], mine[1 - i, rows_of(c), :]], axis=1)
            hi, lo = split(x)
            panel[rows_of(c), i * H : (i + 1) * H] = dot(hi, w_hi) + (dot(hi, w_lo) + dot(lo, w_hi))

    def out_m(c):
        return pltpu.make_async_copy(panel.at[rows_of(c)], matrix_out.at[rows_of(c)], out_sem.at[c])

    def out_v(c):
        return pltpu.make_async_copy(
            panel.at[rows_of(m_chunks + c)], vectors_out.at[rows_of(c)], out_sem.at[m_chunks + c]
        )

    def finish_m(c):
        finish_chunk(c)
        out_m(c).start()

    def finish_v(c):
        receive(0, m_chunks + c).wait_recv()
        receive(1, m_chunks + c).wait_recv()
        finish_chunk(m_chunks + c)
        out_v(c).start()

    each(m_chunks, finish_m)
    each(v_chunks, finish_v)
    each(chunks, lambda c: send(0, c).wait_send())
    each(chunks, lambda c: send(1, c).wait_send())
    each(m_chunks, lambda c: out_m(c).wait())
    each(v_chunks, lambda c: out_v(c).wait())


def solution(mesh):
    n_rows, n_pairs = mesh.shape["rows"], mesh.shape["pairs"]

    def per_device(matrix, vectors):
        m_rows, v_rows = matrix.shape[0], vectors.shape[0]
        rows = m_rows + v_rows
        chunks = rows // CHUNK
        piece = H // n_rows
        dma = pltpu.SemaphoreType.DMA
        return pl.pallas_call(
            functools.partial(kernel, n_rows, n_pairs, m_rows, v_rows),
            out_shape=(
                jax.ShapeDtypeStruct(matrix.shape, F32),
                jax.ShapeDtypeStruct(vectors.shape, F32),
            ),
            in_specs=[pl.BlockSpec(memory_space=pl.ANY)] * 2,
            out_specs=(pl.BlockSpec(memory_space=pl.ANY),) * 2,
            scratch_shapes=[
                pltpu.VMEM((rows, W), F32),
                pltpu.VMEM((2, rows, H), F32),
                pltpu.VMEM((2, rows, H), F32),
                pltpu.VMEM((2, W, W), F32),
                pltpu.VMEM((H, 3 * H), F32),
                pltpu.VMEM((n_rows, piece, 3 * H), F32),
                pltpu.VMEM((H, 3 * H), F32),
                pltpu.VMEM((2, H, H), F32),
                pltpu.VMEM((H, W), F32),
                pltpu.VMEM((n_rows, piece, W), F32),
                pltpu.VMEM((4, H, H), F32),
            ]
            + [pltpu.VMEM((W, H), F32)] * 8
            + [dma((chunks,)), dma((chunks,)), dma((2, chunks)), dma((2, chunks))]
            + [dma((n_rows,))] * 4
            + [dma((2,))] * 2
            + [dma((n_rows,))] * 4,
            compiler_params=pltpu.CompilerParams(
                collective_id=0, has_side_effects=True, vmem_limit_bytes=48 * 2**20
            ),
        )(matrix, vectors)

    spec = P("rows", "pairs")
    return jax.shard_map(per_device, mesh=mesh, in_specs=(spec, spec), out_specs=(spec, spec), check_vma=False)
```

time: 600 us -> 169 us (0.28)
  waiting for transfers between devices: 243 us -> 0 us
  local copies, waits for them, and re-layouts: 170 us -> 6.66 us
  Pallas kernels: 0 us -> 161 us
  matrix products: 111 us -> 0 us
  starting transfers between devices: 29.2 us -> 0 us
  other arithmetic: 25.1 us -> 0 us
  between operations: 14.4 us -> 0.65 us
    pallas_call x0 -> x1, Pallas kernels: none -> 161 us  [per_device(): pl.pallas_call(functools.partial(kernel, n_rows, n_pairs, m_rows, v_rows)...]
    psum x2 -> x0, waiting for transfers between devices: 152 us -> none  [full_gram(): return lax.psum(inner_products(matrix, matrix), 'rows')]
    gather x64 -> x0, local copies, waits for them, and re-layouts: 126 us -> none  [the longest x32 84.6 us: one_step(): diag = jnp.diagonal(current)]
    dot_general x136 -> x0, matrix products: 111 us -> none  [the longest x134 95.7 us: exact_dot(): jnp.dot(left, right, precision=lax.Precision.HIGHEST, preferred_element_t...]
    ppermute x8 -> x0, waiting for transfers between devices: 90.9 us -> none  [shifted(): return lax.ppermute(block, axis, route)]
    ppermute x8 -> x0, starting transfers between devices: 28.9 us -> none  [shifted(): return lax.ppermute(block, axis, route)]
    slice x32 -> x0, local copies, waits for them, and re-layouts: 27.1 us -> none  [one_step(): cross = jnp.diagonal(current[:half, half:])]
    select_n x8 -> x0, other arithmetic: 15.3 us -> none  [the longest x2 6.64 us: per_device(): jnp.where(first, top_a, from_left[0])]
  transfers between devices with their start and end apart: 10 -> 0, of which waited for: 5 -> 0; matrix products, arithmetic and copies ran while one was open for 23% -> 0% of each run, Pallas kernels for 0% -> 0%
where the time goes in v1:
time: 169 us; the launch traced here: 168 us
  Pallas kernels  161 us (95%)
  local copies, waits for them, and re-layouts  6.66 us (4%)
    pallas_call x1, Pallas kernels, per_device(): pl.pallas_call(functools.partial(kernel, n_rows, n_pairs, m_rows, v_rows)...  161 us
    unnamed x4, local copies, waits for them, and re-layouts  6.66 us

profile of v1, /device:TPU:68, one launch (start us, length us, event | category | flops | bytes accessed | tf_op | source)
XLA Modules:
  0.0 168.4 jit_solution(10481240384066928179)
XLA Ops:
  0.6 0.0 copy-start
  0.6 1.2 copy-done
  1.9 161.1 %shard_map.41 = (f32[4096,256]{1,0:T(8,128)}, f32[1024,256]{1,0:T(8,128)S(1)}) custom-call(f32[4096,256]{1,0:T(8,128)} %matrix.1, f32[1024,256]{1,0:T(8,128)S(1)} %copy-done), custom_call_target="tpu_custom_call" | custom-call | tf_op jit(solution)/shard_map/pallas_call | solution.py:431
  162.9 4.5 %copy.6 = f32[4096,256]{1,0:T(8,128)} copy(f32[4096,256]{1,0:T(8,128)} %get-tuple-element.4) | data formatting | bytes 8388608
  167.4 1.0 copy.7
Async XLA Ops:
  0.6 1.2 copy-start

commit v2 on v1

v2 whole, which is shorter than its diff:
```python
import functools

import jax
import jax.numpy as jnp
from jax import lax
from jax.experimental import pallas as pl
from jax.experimental.pallas import tpu as pltpu
from jax.sharding import PartitionSpec as P

STEPS = 16
H = 128
W = 2 * H
CHUNK = 256
MESH = pl.DeviceIdType.MESH
F32 = jnp.float32
BF16 = jnp.bfloat16


def iota(shape, axis):
    return lax.broadcasted_iota(jnp.int32, shape, axis)


def split(v):
    hi = v.astype(BF16)
    return hi, (v - hi.astype(F32)).astype(BF16)


def split3(v):
    hi = v.astype(BF16)
    rest = v - hi.astype(F32)
    mid = rest.astype(BF16)
    return hi, mid, (rest - mid.astype(F32)).astype(BF16)


def dot(a, b):
    return jnp.dot(a, b, preferred_element_type=F32)


def dot_t(a, b):
    return lax.dot_general(a, b, (((0,), (0,)), ((), ())), preferred_element_type=F32)


def diag_row(block):
    lane = iota((8, H), 1)
    sub = iota((8, H), 0)
    parts = []
    for g in range(4):
        acc = block[32 * g : 32 * g + 8]
        for i in range(4 * g + 1, 4 * g + 4):
            acc = jnp.where(lane // 8 == i, block[8 * i : 8 * i + 8], acc)
        parts.append(acc)
    low = jnp.where(lane < 32, parts[0], parts[1])
    high = jnp.where(lane < 96, parts[2], parts[3])
    both = jnp.where(lane < 64, low, high)
    return jnp.sum(jnp.where(lane % 8 == sub, both, 0.0), axis=0, keepdims=True)


def angles(x, y):
    m = jnp.maximum(jnp.abs(x), jnp.abs(y))
    g = pl.reciprocal(m, approx=True)
    xs = x * g
    ys = y * g
    s = xs * xs + ys * ys
    r = s * lax.rsqrt(s)
    h = r + jnp.abs(xs)
    w = lax.rsqrt(2.0 * r * h)
    big = h * w
    small = jnp.abs(ys) * w
    flat = x >= 0.0
    none = m == 0.0
    cs = jnp.where(none, 1.0, jnp.where(flat, big, small))
    sn = jnp.where(none, 0.0, jnp.where(flat, small, big))
    return cs, jnp.where(y < 0.0, -sn, sn)


def lane_move(left, right):
    lane0 = iota(left.shape, 1) == 0
    rolled = pltpu.roll(jnp.where(lane0, right, left), 1, 1)
    new_left = jnp.where(lane0, left, rolled)
    new_right = pltpu.roll(jnp.where(lane0, rolled, right), H - 1, 1)
    return new_left, new_right


def as_columns(cs, sn):
    t = jnp.transpose(jnp.where(iota((H, H), 0) < H // 2, cs, sn))
    o = pltpu.roll(t, H // 2, 1)
    near = iota((H, H), 1) < H // 2
    return jnp.where(near, t, o), jnp.where(near, o, t)


def store_rows(ref, up, lo):
    ref[H - 1 : W - 1, :] = lo
    ref[1:H, :] = up[0 : H - 1]
    ref[0:1, :] = up[0:1]
    ref[1:2, :] = lo[0:1]
    ref[W - 1 : W, :] = up[H - 1 : H]


def jacobi_start(state, a, c, c_t, b):
    gl, gr, ql, qr = state
    gl[0:H, :] = a
    gl[H:W, :] = c_t
    gr[0:H, :] = c
    gr[H:W, :] = b
    ql[...] = (iota((W, H), 0) == iota((W, H), 1)).astype(F32)
    qr[...] = (iota((W, H), 0) == iota((W, H), 1) + H).astype(F32)


def jacobi_step(state):
    gl, gr, ql, qr = state
    a, d, c, b = gl[0:H], gl[H:W], gr[0:H], gr[H:W]
    cs, sn = angles(diag_row(a) - diag_row(b), 2.0 * diag_row(c))
    cc, sc = as_columns(cs, sn)
    a, c = lane_move(a * cs + c * sn, c * cs - a * sn)
    d, b = lane_move(d * cs + b * sn, b * cs - d * sn)
    store_rows(gl, a * cc + d * sc, d * cc - a * sc)
    store_rows(gr, c * cc + b * sc, b * cc - c * sc)
    left, right = ql[...], qr[...]
    left, right = lane_move(left * cs + right * sn, right * cs - left * sn)
    ql[...] = left
    qr[...] = right


def home():
    j = iota((W, W), 1)
    at = jnp.where(j < H - STEPS, j + STEPS, 3 * H - STEPS - 1 - j)
    at = jnp.where(j >= H, H + STEPS - j, at)
    at = jnp.where(j >= H + STEPS, j - STEPS, at)
    at = jnp.where(j == 0, 0, at)
    return (iota((W, W), 0) == at).astype(F32).astype(BF16)


def basis_split(state, sel):
    ql, qr = state[2], state[3]
    lh, ll = split(ql[...])
    rh, rl = split(qr[...])
    high = dot(lh, sel[0:H]) + dot(rh, sel[H:W])
    low = dot(ll, sel[0:H]) + dot(rl, sel[H:W])
    return high.astype(BF16), low.astype(BF16)


def gram_blocks(state, sel):
    gl, gr = state[0], state[1]
    moved = sum(dot(l, sel[0:H]) + dot(r, sel[H:W]) for l, r in zip(split3(gl[...]), split3(gr[...])))
    parts = split3(moved)
    top = sum(dot_t(sel[:, 0:H], p[:, 0:H]) for p in parts)
    bottom = sum(dot_t(sel[:, H:W], p[:, H:W]) for p in parts)
    return top, bottom


def kernel(
    n_rows, n_pairs, m_rows, v_rows,
    matrix, vectors, matrix_out, vectors_out,
    panel, other, xy, near, fwd, far, acc, gs, rs1, part1, cross1, ag1, diag, far_diag, rs2src, rs2, part2, cross2, ag2,
    a_gl, a_gr, a_ql, a_qr, b_gl, b_gr, b_ql, b_qr,
    load_sem, out_sem, raw_send, raw_recv, fwd_send, sib_send, far_recv, rs1_send, rs1_recv, ag1_send, ag1_recv,
    rs2_send, rs2_recv, ag2_send, ag2_recv, x1_send, x1_recv, x2_send, x2_recv, dg_send, dg_recv,
):
    me = lax.axis_index("rows")
    k = lax.axis_index("pairs")
    m_chunks, v_chunks = m_rows // CHUNK, v_rows // CHUNK
    chunks = m_chunks + v_chunks
    n_y = n_rows // 2
    y = lax.rem(me, n_y)
    across = lax.rem(me + n_y, n_rows)
    piece = H // n_y
    mine_rows = pl.ds(pl.multiple_of(y * piece, piece), piece)

    side = lax.rem(k // 2, 2)
    low = side == 0
    step = jnp.where(low, 2, -2)
    partner = k + step
    sibling = k + 1 - 2 * lax.rem(k, 2)
    begins, ends = k < 4, k >= n_pairs - 4
    has_fwd = jnp.where(low, jnp.where(ends, 0, 1), jnp.where(begins, 0, 1)) == 1
    has_sib = jnp.where(low, jnp.where(begins, 1, 0), jnp.where(ends, 1, 0)) == 1
    fwd_to = jnp.where(has_fwd, k + 2 * step, sibling)
    x_is_top = jnp.where(low, jnp.where(k == 0, 0, 1), 0) == 1
    px_is_top = jnp.where(low, 0, jnp.where(partner == 0, 0, 1)) == 1
    far_first = jnp.where(low, jnp.where(k == 0, 0, 1), jnp.where(k == n_pairs - 1, 1, 0)) == 1
    far_takes_top = jnp.where(low, jnp.where(k == 1, 0, 1), jnp.where(k == n_pairs - 1, 1, 0)) == 1

    def rows_of(c):
        return pl.ds(pl.multiple_of(c * CHUNK, CHUNK), CHUNK)

    def each(n, body, start=0):
        lax.fori_loop(start, n, lambda i, carry: (body(i), carry)[1], 0)

    def load_m(c):
        return pltpu.make_async_copy(matrix.at[rows_of(c)], panel.at[rows_of(c)], load_sem.at[c])

    def load_v(c):
        at = rows_of(m_chunks + c)
        return pltpu.make_async_copy(vectors.at[rows_of(c)], panel.at[at], load_sem.at[m_chunks + c])

    def raw_m(c):
        return pltpu.make_async_remote_copy(
            src_ref=matrix.at[rows_of(c)], dst_ref=other.at[rows_of(c)], send_sem=raw_send.at[c],
            recv_sem=raw_recv.at[c], device_id=(me, partner), device_id_type=MESH,
        )

    def raw_v(c):
        at = rows_of(m_chunks + c)
        return pltpu.make_async_remote_copy(
            src_ref=vectors.at[rows_of(c)], dst_ref=other.at[at], send_sem=raw_send.at[m_chunks + c],
            recv_sem=raw_recv.at[m_chunks + c], device_id=(me, partner), device_id_type=MESH,
        )

    def raw_in(c):
        return pltpu.make_async_remote_copy(
            src_ref=panel.at[rows_of(c)], dst_ref=other.at[rows_of(c)], send_sem=raw_send.at[c],
            recv_sem=raw_recv.at[c], device_id=(me, partner), device_id_type=MESH,
        )

    def forward(c):
        return pltpu.make_async_remote_copy(
            src_ref=fwd.at[rows_of(c)], dst_ref=far.at[rows_of(c)], send_sem=fwd_send.at[c],
            recv_sem=far_recv.at[c], device_id=(me, fwd_to), device_id_type=MESH,
        )

    def to_sibling(c):
        return pltpu.make_async_remote_copy(
            src_ref=xy.at[1, rows_of(c)], dst_ref=far.at[rows_of(c)], send_sem=sib_send.at[c],
            recv_sem=far_recv.at[c], device_id=(me, sibling), device_id_type=MESH,
        )

    each(m_chunks, lambda c: load_m(c).start())
    each(v_chunks, lambda c: load_v(c).start())

    barrier = pltpu.get_barrier_semaphore()

    def greet(row, pair):
        pl.semaphore_signal(barrier, inc=1, device_id=(row, pair), device_id_type=MESH)

    def y_peer(d):
        return lax.rem(y + d, n_y)

    def peer(d):
        return me - y + y_peer(d)

    for d in range(1, n_y):
        greet(peer(d), k)
    greet(across, k)
    greet(across, partner)
    greet(me, partner)
    greet(me, sibling)

    @pl.when(jnp.logical_not(begins))
    def _():
        greet(me, k - 4)

    @pl.when(jnp.logical_not(ends))
    def _():
        greet(me, k + 4)

    pl.semaphore_wait(barrier, n_y + 3 + jnp.where(begins, 0, 1) + jnp.where(ends, 0, 1))
    raw_m(0).start()
    raw_m(1).start()

    acc[...] = jnp.zeros_like(acc)

    def gram_chunk(c):
        load_m(c).wait()
        hi, lo = split(panel[rows_of(c), :])
        acc[0] += dot_t(hi, hi)
        acc[1] += dot_t(hi, lo)

    each(m_chunks, gram_chunk)
    hl = acc[1]
    full = acc[0] + (hl + jnp.transpose(hl))
    gs[:, 0:H] = full[0:H, 0:H]
    gs[:, H:W] = full[0:H, H:W]
    gs[:, W:] = full[H:W, H:W]

    def scatter(src, dst, send, recv):
        copies = []
        for d in range(1, n_y):
            rows = pl.ds(pl.multiple_of(y_peer(d) * piece, piece), piece)
            copies.append(
                pltpu.make_async_remote_copy(
                    src_ref=src.at[rows], dst_ref=dst.at[d - 1], send_sem=send.at[d], recv_sem=recv.at[d],
                    device_id=(peer(d), k), device_id_type=MESH,
                )
            )
        for copy in copies:
            copy.start()
        for copy in copies:
            copy.wait()
        total = src[mine_rows, :]
        for d in range(1, n_y):
            total = total + dst[d - 1]
        return total

    def gather(part, send, recv):
        copies = []
        for d in range(1, n_y):
            copies.append(
                pltpu.make_async_remote_copy(
                    src_ref=part, dst_ref=part, send_sem=send.at[d], recv_sem=recv.at[d],
                    device_id=(peer(d), k), device_id_type=MESH,
                )
            )
        for copy in copies:
            copy.start()
        for copy in copies:
            copy.wait()

    part1[...] = scatter(gs, rs1, rs1_send, rs1_recv)
    copies = []
    for i, to in enumerate(((across, k), (me, partner), (across, partner))):
        copies.append(
            pltpu.make_async_remote_copy(
                src_ref=part1, dst_ref=cross1.at[i], send_sem=x1_send.at[i], recv_sem=x1_recv.at[i],
                device_id=to, device_id_type=MESH,
            )
        )
    for copy in copies:
        copy.start()
    for copy in copies:
        copy.wait()
    each(m_chunks, lambda c: raw_m(c).start(), start=2)
    raw_v(0).start()
    ag1[0, mine_rows, :] = part1[...] + cross1[0]
    ag1[1, mine_rows, :] = cross1[1] + cross1[2]
    gather(ag1.at[:, mine_rows], ag1_send, ag1_recv)

    state_a = (a_gl, a_gr, a_ql, a_qr)
    state_b = (b_gl, b_gr, b_ql, b_qr)
    for i, state in enumerate((state_a, state_b)):
        c1 = ag1[i, :, H:W]
        jacobi_start(state, ag1[i, :, 0:H], c1, jnp.transpose(c1), ag1[i, :, W:])

    def both(t):
        jacobi_step(state_a)
        jacobi_step(state_b)

    each(STEPS, both)
    sel = home()

    def xy_order(state, top_first):
        parts = []
        for q in basis_split(state, sel):
            q = q.astype(F32)
            left = jnp.where(top_first, q[:, 0:H], q[:, H:W])
            right = jnp.where(top_first, q[:, H:W], q[:, 0:H])
            parts.append(jnp.concatenate([left, right], axis=1).astype(BF16))
        return parts

    def product(x, w_hi, w_lo):
        hi, lo = split(x)
        return dot(hi, w_hi) + (dot(hi, w_lo) + dot(lo, w_hi))

    each(v_chunks, lambda c: load_v(c).wait())
    q_hi, q_lo = xy_order(state_a, x_is_top)

    def rotate_mine(c):
        new = product(panel[rows_of(c), :], q_hi, q_lo)
        xy[0, rows_of(c), :] = new[:, 0:H]
        xy[1, rows_of(c), :] = new[:, H:W]

        @pl.when(has_sib)
        def _():
            to_sibling(c).start()

    each(chunks, rotate_mine)

    for i, (state, top_first) in enumerate(((state_a, x_is_top), (state_b, px_is_top))):
        top, bottom = gram_blocks(state, sel)
        diag[2 * i] = jnp.where(top_first, top, bottom)
        diag[2 * i + 1] = jnp.where(top_first, bottom, top)

    def send_diag(i, to):
        return pltpu.make_async_remote_copy(
            src_ref=diag.at[2 * i + 1], dst_ref=far_diag, send_sem=dg_send.at[i], recv_sem=dg_recv,
            device_id=(me, to), device_id_type=MESH,
        )

    @pl.when(has_sib)
    def _():
        send_diag(0, sibling).start()

    @pl.when(has_fwd)
    def _():
        send_diag(1, fwd_to).start()

    p_hi, p_lo = xy_order(state_b, px_is_top)

    def rotate_other(c):
        raw_in(c).wait_recv()
        new = product(other[rows_of(c), :], p_hi, p_lo)
        fwd[rows_of(c), :] = new[:, H:W]
        near[rows_of(c), :] = new[:, 0:H]

        @pl.when(has_fwd)
        def _():
            forward(c).start()

    acc[...] = jnp.zeros_like(acc)

    def cross(i, half, c):
        x = jnp.concatenate(split(xy[i, rows_of(c), :]), axis=1)
        y = jnp.concatenate(split(half[rows_of(c), :]), axis=1)
        acc[i] += dot_t(x, y)

    def far_cross(c):
        forward(c).wait_recv()
        cross(1, far, c)

    def round_chunk(c):
        rotate_other(c)
        cross(0, near, c)

        @pl.when(c > 0)
        def _():
            far_cross(c - 1)

    each(m_chunks, round_chunk)
    far_cross(m_chunks - 1)
    for i in range(2):
        z = acc[i]
        rs2src[:, i * H : (i + 1) * H] = z[0:H, 0:H] + ((z[0:H, H:W] + z[H:W, 0:H]) + z[H:W, H:W])
    part2[...] = scatter(rs2src, rs2, rs2_send, rs2_recv)
    copy = pltpu.make_async_remote_copy(
        src_ref=part2, dst_ref=cross2, send_sem=x2_send, recv_sem=x2_recv, device_id=(across, k), device_id_type=MESH
    )
    copy.start()
    each(v_chunks, lambda c: raw_v(c).start(), start=1)
    copy.wait()
    ag2[mine_rows, :] = part2[...] + cross2[...]
    gather(ag2.at[mine_rows], ag2_send, ag2_recv)
    send_diag(0, sibling).wait_recv()

    def start_pair(state, mine_first, mine, theirs, z):
        z_t = jnp.transpose(z)
        jacobi_start(
            state, jnp.where(mine_first, mine, theirs), jnp.where(mine_first, z, z_t),
            jnp.where(mine_first, z_t, z), jnp.where(mine_first, theirs, mine),
        )

    start_pair(state_a, low, diag[0], diag[2], ag2[:, 0:H])
    start_pair(state_b, jnp.logical_not(far_first), diag[1], far_diag[...], ag2[:, H:W])
    each(STEPS // 2, both)
    rotate_other(m_chunks)
    each(STEPS // 2, both)
    each(chunks, rotate_other, start=m_chunks + 1)

    def weights(state, take_top, theirs_first):
        parts = []
        for q in basis_split(state, sel):
            q = q.astype(F32)
            q = jnp.where(take_top, q[:, 0:H], q[:, H:W])
            up = jnp.where(theirs_first, q[0:H], q[H:W])
            down = jnp.where(theirs_first, q[H:W], q[0:H])
            parts.append(jnp.concatenate([up, down], axis=0).astype(BF16))
        return parts

    wn_hi, wn_lo = weights(state_a, jnp.logical_not(low), jnp.logical_not(low))
    wf_hi, wf_lo = weights(state_b, far_takes_top, far_first)
    near_cols = pl.ds(pl.multiple_of((1 - side) * H, H), H)
    far_cols = pl.ds(pl.multiple_of(side * H, H), H)

    def finish_chunk(c):
        x = jnp.concatenate([near[rows_of(c), :], xy[0, rows_of(c), :]], axis=1)
        panel[rows_of(c), near_cols] = product(x, wn_hi, wn_lo)
        x = jnp.concatenate([far[rows_of(c), :], xy[1, rows_of(c), :]], axis=1)
        panel[rows_of(c), far_cols] = product(x, wf_hi, wf_lo)

    def out_m(c):
        return pltpu.make_async_copy(panel.at[rows_of(c)], matrix_out.at[rows_of(c)], out_sem.at[c])

    def out_v(c):
        return pltpu.make_async_copy(
            panel.at[rows_of(m_chunks + c)], vectors_out.at[rows_of(c)], out_sem.at[m_chunks + c]
        )

    def finish_m(c):
        finish_chunk(c)
        out_m(c).start()

    def finish_v(c):
        forward(m_chunks + c).wait_recv()
        finish_chunk(m_chunks + c)
        out_v(c).start()

    each(m_chunks, finish_m)
    each(v_chunks, finish_v)

    each(m_chunks, lambda c: raw_m(c).wait_send())
    each(v_chunks, lambda c: raw_v(c).wait_send())

    @pl.when(has_fwd)
    def _():
        each(chunks, lambda c: forward(c).wait_send())
        send_diag(1, fwd_to).wait_send()

    @pl.when(has_sib)
    def _():
        each(chunks, lambda c: to_sibling(c).wait_send())
        send_diag(0, sibling).wait_send()

    each(m_chunks, lambda c: out_m(c).wait())
    each(v_chunks, lambda c: out_v(c).wait())


def solution(mesh):
    n_rows, n_pairs = mesh.shape["rows"], mesh.shape["pairs"]

    def per_device(matrix, vectors):
        m_rows, v_rows = matrix.shape[0], vectors.shape[0]
        rows = m_rows + v_rows
        chunks = rows // CHUNK
        n_y = n_rows // 2
        piece = H // n_y
        dma = pltpu.SemaphoreType.DMA
        vmem = [
            (rows, W), (rows, W), (2, rows, H), (rows, H), (rows, H), (rows, H), (2, W, W),
            (H, 3 * H), (n_y - 1, piece, 3 * H), (piece, 3 * H), (3, piece, 3 * H), (2, H, 3 * H),
            (4, H, H), (H, H), (H, W), (n_y - 1, piece, W), (piece, W), (piece, W), (H, W),
        ] + [(W, H)] * 8
        sems = [chunks] * 7 + [n_y] * 8 + [3, 3, None, None, 2, None]
        return pl.pallas_call(
            functools.partial(kernel, n_rows, n_pairs, m_rows, v_rows),
            out_shape=(
                jax.ShapeDtypeStruct(matrix.shape, F32),
                jax.ShapeDtypeStruct(vectors.shape, F32),
            ),
            in_specs=[pl.BlockSpec(memory_space=pl.ANY)] * 2,
            out_specs=(pl.BlockSpec(memory_space=pl.ANY),) * 2,
            scratch_shapes=[pltpu.VMEM(shape, F32) for shape in vmem]
            + [dma if n is None else dma((n,)) for n in sems],
            compiler_params=pltpu.CompilerParams(
                collective_id=0, has_side_effects=True, vmem_limit_bytes=60 * 2**20
            ),
        )(matrix, vectors)

    spec = P("rows", "pairs")
    return jax.shard_map(per_device, mesh=mesh, in_specs=(spec, spec), out_specs=(spec, spec), check_vma=False)
```

time: 169 us -> 149 us (0.88)
  Pallas kernels: 161 us -> 143 us
    pallas_call x1, Pallas kernels: 161 us -> 143 us  [per_device(): pl.pallas_call(functools.partial(kernel, n_rows, n_pairs, m_rows, v_rows)...]
where the time goes in v2:
time: 149 us
  Pallas kernels  143 us (96%)
  local copies, waits for them, and re-layouts  5.53 us (4%)
    pallas_call x1, Pallas kernels, per_device(): pl.pallas_call(functools.partial(kernel, n_rows, n_pairs, m_rows, v_rows)...  143 us
    unnamed x4, local copies, waits for them, and re-layouts  5.53 us

profile of v2, /device:TPU:68, one launch (start us, length us, event | category | flops | bytes accessed | tf_op | source)
XLA Modules:
  0.0 149.1 jit_solution(256140927126566616)
XLA Ops:
  0.6 143.0 %shard_map.41 = (f32[4096,256]{1,0:T(8,128)}, f32[1024,256]{1,0:T(8,128)}) custom-call(f32[4096,256]{1,0:T(8,128)} %matrix.1, f32[1024,256]{1,0:T(8,128)} %vectors.1), custom_call_target="tpu_custom_call" | custom-call | tf_op jit(solution)/shard_map/pallas_call | solution.py:521
  143.6 0.0 copy-start
  143.6 4.6 %copy.6 = f32[4096,256]{1,0:T(8,128)} copy(f32[4096,256]{1,0:T(8,128)} %get-tuple-element.4) | data formatting | bytes 8388608
  148.2 0.0 copy-done
  148.2 1.0 copy.7
Async XLA Ops:
  143.6 4.6 %copy-start = (f32[1024,256]{1,0:T(8,128)S(1)}, f32[1024,256]{1,0:T(8,128)}, u32[]{:S(2)}) copy-start(f32[1024,256]{1,0:T(8,128)} %get-tuple-element.5) | copy-start | bytes 3145732
